TPU v7x, 32 devices: a whole 2x2x4 slice. The times are simulated.
32 devices in a mesh: groups: 2 (over x), attn: 16 (over z, y, core).
Axes of the slice: x: 2, y: 2, z: 4, core: 2. Of those that a mesh axis runs over, the one named last changes fastest.
Arguments:
- queries: bfloat16 [256, 6144], P(('groups', 'attn')), parts along dimension 0, may hold values from -6 to 6
- kv_cache: bfloat16 [256, 48, 2048], P(('groups', 'attn')), parts along dimension 0, may hold values from -6 to 6
- lengths: int32 [256], P(('groups', 'attn')), parts along dimension 0, may hold values from 2 to 48, as said below
- handoff: int32 [32, 2], P(('groups', 'attn')), parts along dimension 0, may hold values from 0 to 7, as said below
- routes: int32 [256, 1], P(('groups', 'attn')), parts along dimension 0, may hold values from 0 to 1; in each aligned block of 8 rows (0 to 7, 8 to 15, ...) at most 6 rows name the same one
- norm_gain: bfloat16 [6144], replicated, may hold values from 0.099609375 to 1.8984375
- router: bfloat16 [6144, 2], replicated, may hold values from -0.078125 to 0.078125
- gate_proj: bfloat16 [6144, 16384], P(None, 'attn'), may hold values from -0.078125 to 0.078125
- up_proj: bfloat16 [6144, 16384], P(None, 'attn'), may hold values from -0.078125 to 0.078125
- down_proj: bfloat16 [16384, 6144], P('attn'), may hold values from -0.0625 to 0.0625
Outputs:
- mixed: bfloat16 [256, 6144], P(('groups', 'attn')), parts along dimension 0
There are 2 independent parts, one for each index of `groups`. A program takes and returns all parts, laid end to end along the dimension named above; an argument that names none is the same for every part. Nothing has to cross between parts.
Inputs may be any that keep to these rules, and one draw needn't show every extreme that they name: `lengths`: some request has 48 cached positions. `handoff`: each row names 2 different local slots; the requests in them go to the device whose index differs in the highest bit. `routes`: in each aligned block of 8 rows (the slots of one device) no expert is named by more than 6 rows.
All inputs are finite; a program needn't handle non-finite values.
Results may differ from a plain program's by a relative error of at most 0.014.
Values may be sent and summed in bfloat16 or wider, within the bound.
A program may use at most 128 MiB of HBM per device.

v0:
```python
import jax
import jax.numpy as jnp
from jax import lax
from jax.sharding import PartitionSpec as P

HQ = 48
KVH = 8
HD = 128
EXPERTS = 2
LMAX = 48
CAP = 6


def partner(array, axis, distance):
    return lax.ppermute(array, axis, [(i, i ^ 1 << distance) for i in range(lax.axis_size(axis))])


def attend(query_rows, cache_rows, length_rows):
    total_rows = query_rows.shape[0]
    width_kv = KVH * HD
    heads_q = query_rows.reshape(total_rows, KVH, HQ // KVH, HD)
    keys_all = cache_rows[:, :, :width_kv].reshape(total_rows, LMAX, KVH, HD)
    values_all = cache_rows[:, :, width_kv:].reshape(total_rows, LMAX, KVH, HD)
    scores = jnp.einsum(
        "rkgd,rtkd->rkgt", heads_q, keys_all, preferred_element_type=jnp.float32
    ) * HD ** (-0.5)
    visible = jnp.arange(LMAX, dtype=jnp.int32)[None, :] < length_rows[:, None]
    scores = jnp.where(visible[:, None, None, :], scores, -jnp.inf)
    highest = jnp.max(scores, axis=-1, keepdims=True)
    weights = jnp.exp(scores - highest)
    weights = (weights / jnp.sum(weights, axis=-1, keepdims=True)).astype(jnp.bfloat16)
    mixed_heads = jnp.einsum(
        "rkgt,rtkd->rkgd", weights, values_all, preferred_element_type=jnp.float32
    )
    return mixed_heads.reshape(total_rows, HQ * HD).astype(jnp.bfloat16)


def body(
    queries, kv_cache, lengths, handoff, routes, norm_gain, router, gate_proj, up_proj, down_proj
):
    ranks = lax.axis_size("attn")
    picks = handoff[0]
    highest_bit = ranks.bit_length() - 2
    moved = partner(
        (queries[picks], kv_cache[picks], lengths[picks].astype(jnp.bfloat16)), "attn", highest_bit
    )
    attended = attend(
        queries.at[picks].set(moved[0]),
        kv_cache.at[picks].set(moved[1]),
        lengths.at[picks].set(moved[2].astype(jnp.int32)),
    )
    attended_f = attended.astype(jnp.float32)
    scale_rows = lax.rsqrt(jnp.mean(attended_f * attended_f, axis=-1, keepdims=True) + 1e-05)
    normed = (attended_f * scale_rows * norm_gain.astype(jnp.float32)).astype(jnp.bfloat16)
    logits = jnp.dot(normed, router, preferred_element_type=jnp.float32)
    chosen_logit = jnp.take_along_axis(logits, routes, axis=1)
    gate_prob = 1.0 / jnp.sum(jnp.exp(logits - chosen_logit), axis=1)
    chosen_expert = routes[:, 0]
    row_order = jnp.arange(chosen_expert.shape[0], dtype=jnp.int32)
    earlier = (chosen_expert[:, None] == chosen_expert[None, :]) & (
        row_order[None, :] < row_order[:, None]
    )
    slot_index = jnp.sum(earlier.astype(jnp.int32), axis=1)
    target = chosen_expert * CAP + slot_index
    selector = (jnp.arange(EXPERTS * CAP, dtype=jnp.int32)[:, None] == target[None, :]).astype(
        jnp.bfloat16
    )
    width = normed.shape[1]
    dispatch = (
        jnp.dot(selector, normed, preferred_element_type=jnp.float32)
        .astype(jnp.bfloat16)
        .reshape(EXPERTS, CAP, width)
    )
    group_size = ranks // EXPERTS
    mine = lax.axis_index("attn") // group_size
    own_rows = lax.dynamic_index_in_dim(
        lax.all_gather(dispatch[None], "attn", axis=0, tiled=True), mine, 1, keepdims=False
    )
    flat = own_rows.reshape(-1, width)
    gated = jnp.dot(flat, gate_proj, preferred_element_type=jnp.float32)
    upward = jnp.dot(flat, up_proj, preferred_element_type=jnp.float32)
    hidden = (jax.nn.silu(gated) * upward).astype(jnp.bfloat16)
    partial_out = jnp.dot(hidden, down_proj, preferred_element_type=jnp.float32).astype(
        jnp.bfloat16
    )
    partials = partial_out.reshape(own_rows.shape)
    received = lax.all_to_all(partials, "attn", split_axis=0, concat_axis=0, tiled=True)
    summed = received.astype(jnp.float32).reshape(EXPERTS, group_size, CAP, width).sum(axis=1)
    expert_value = jnp.take(summed.reshape(EXPERTS * CAP, width), target, axis=0)
    return (attended_f + gate_prob[:, None] * expert_value).astype(jnp.bfloat16)


def solution(mesh):
    return jax.shard_map(
        body,
        mesh=mesh,
        in_specs=(
            P(("groups", "attn"), None),
            P(("groups", "attn"), None, None),
            P(("groups", "attn")),
            P(("groups", "attn"), None),
            P(("groups", "attn"), None),
            P(),
            P(),
            P(None, "attn"),
            P(None, "attn"),
            P("attn", None),
        ),
        out_specs=P(("groups", "attn"), None),
        check_vma=False,
    )
```

profile of v0, /device:TPU:13, one launch (start us, length us, event | category | flops | bytes accessed | tf_op | source)
XLA Modules:
  0.0 160.4 jit_solution(3269935596654304683)
XLA Ops:
  6.5 0.7 copy.46
  7.2 0.9 copy.44
  8.1 1.4 copy.45
  9.6 0.6 gather_fusion
  10.2 2.3 %collective-permute-start = (bf16[2]{0:T(256)(128)(2,1)S(1)}, bf16[2]{0:T(256)(128)(2,1)S(1)}, u32[]{:S(2)}, u32[]{:S(2)}) collective-permute-start(bf16[2]{0:T(256)(128)(2,1)S(1)} %convert_element_type.46), channel_id=1, source_target_pairs={{0,8},{1,9},{2,10},{3,11},{4,12},{5,13},{6,14},{7,15},{8,0},{9,1},... | collective-permute-start | bytes 20 | tf_op jit(solution)/shard_map/ppermute | solution.py:15
  12.5 0.6 gather_fusion.1
  13.8 2.4 %collective-permute-start.2 = (bf16[2,48,2048]{2,1,0:T(8,128)(2,1)S(1)}, bf16[2,48,2048]{2,1,0:T(8,128)(2,1)S(1)}, u32[]{:S(2)}, u32[]{:S(2)}) collective-permute-start(bf16[2,48,2048]{2,1,0:T(8,128)(2,1)S(1)} %gather_fusion.2), channel_id=1, source_target_pairs={{0,8},{1,9},{2,10},{3,11},{4,12},{5,13},{6,14},{7,15},{8,0},{9,1},... | collective-permute-start | bytes 1179656 | tf_op jit(solution)/shard_map/ppermute | solution.py:15
  16.4 0.6 scatter_fusion
  17.1 0.7 scatter_fusion.1
  17.8 15.5 %collective-permute-done.2 = bf16[2,48,2048]{2,1,0:T(8,128)(2,1)S(1)} collective-permute-done((bf16[2,48,2048]{2,1,0:T(8,128)(2,1)S(1)}, bf16[2,48,2048]{2,1,0:T(8,128)(2,1)S(1)}, u32[]{:S(2)}, u32[]{:S(2)}) %collective-permute-start.2) | collective-permute-done | bytes 393248 | tf_op jit(solution)/shard_map/ppermute | solution.py:15
  33.4 0.7 scatter_fusion.2
  34.9 1.0 multiply_reduce_fusion
  36.3 0.8 copy.22
  37.2 43.0 %all-gather.2.cloned.1.call-done = bf16[16,2,6,6144]{3,1,2,0:T(2,128)(2,1)} async-done(((bf16[1,2,6,6144]{3,1,2,0:T(2,128)(2,1)}), bf16[16,2,6,6144]{3,1,2,0:T(2,128)(2,1)}) %all-gather.2.cloned.1.call-update) | async-done | bytes 2359312 | tf_op jit(solution)/shard_map/all_gather | solution.py:77
  80.2 8.8 %dynamic-slice_reduce_fusion = bf16[16,6,6144]{2,1,0:T(8,128)(2,1)S(1)} fusion(bf16[16,2,6,6144]{3,1,2,0:T(2,128)(2,1)} %all-gather.2.cloned.1.call-done, s32[]{:T(128)S(6)} %select_n.55), kind=kLoop, calls=%fused_computation.12 | loop fusion | bytes 2359300 | tf_op jit(solution)/shard_map/jit(dynamic_index_in_dim)/dynamic_slice | solution.py:76
  89.0 0.6 reshape.124
  89.7 6.7 %fusion.35 = f32[96,1024]{1,0:T(8,128)S(1)} fusion(bf16[96,6144]{1,0:T(8,128)(2,1)S(1)} %reshape.124, bf16[6144,1024]{1,0:T(8,128)(2,1)} %param.17), kind=kOutput, calls=%fused_computation.69 | convolution fusion | flops 1207959552 | bytes 14155776 | tf_op jit(solution)/shard_map/dot_general | solution.py:80
  96.4 12.4 %convolution_convert_fusion = bf16[96,6144]{1,0:T(8,128)(2,1)S(1)} fusion(bf16[1024,6144]{1,0:T(8,128)(2,1)} %param.19, bf16[96,6144]{1,0:T(8,128)(2,1)S(1)} %reshape.124, bf16[6144,1024]{1,0:T(8,128)(2,1)} %param.18, f32[96,1024]{1,0:T(8,128)S(1)} %fusion.35), kind=kOutput, calls=%fused_computation.9 | convolution fusion | flops 2417098752 | bytes 27918336 | tf_op jit(solution)/shard_map/dot_general | solution.py:83
  108.8 1.4 reshape.125
  110.2 5.4 %all-to-all-start = ((bf16[16,6,6144]{2,1,0:T(8,128)(2,1)}), bf16[16,6,6144]{2,1,0:T(8,128)(2,1)S(1)}, u32[]{:S(2)}, u32[]{:S(2)}) async-start(bf16[16,6,6144]{2,1,0:T(8,128)(2,1)} %reshape.125), calls=%async_computation | async-start | bytes 3145728 | tf_op jit(solution)/shard_map/all_to_all | solution.py:87
  115.9 0.7 gather_fusion.4
  116.6 35.2 %all-to-all-done = bf16[16,6,6144]{2,1,0:T(8,128)(2,1)S(1)} async-done(((bf16[16,6,6144]{2,1,0:T(8,128)(2,1)}), bf16[16,6,6144]{2,1,0:T(8,128)(2,1)S(1)}, u32[]{:S(2)}, u32[]{:S(2)}) %all-to-all-start) | async-done | bytes 1179680 | tf_op jit(solution)/shard_map/all_to_all | solution.py:87
  152.2 0.6 gather_fusion.3
  152.8 0.7 add_convert_fusion
  (42 shorter events, 2.9 us)
Async XLA Ops:
  6.5 109.2 %copy-start = (bf16[6144,2]{0,1:T(2,128)(2,1)S(1)}, bf16[6144,2]{0,1:T(2,128)(2,1)}, u32[]{:S(2)}) copy-start(bf16[6144,2]{0,1:T(2,128)(2,1)} %param.16) | copy-start | bytes 73732
  6.5 73.6 %all-gather.2.cloned.1.call-start = ((), (), s32[]{:S(2)}) async-start(), calls=%async_computation.1 | async-start | bytes 2506752 | tf_op jit(solution)/shard_map/all_gather | solution.py:77
  8.1 1.5 copy-start.3
  8.1 8.1 %copy-start.2 = (s32[8,1]{0,1:T(1,128)S(1)}, s32[8,1]{0,1:T(1,128)}, u32[]{:S(2)}) copy-start(s32[8,1]{0,1:T(1,128)} %param.14) | copy-start | bytes 100
  8.1 8.3 %copy-start.1 = (bf16[6144]{0:T(1024)(128)(2,1)S(1)}, bf16[6144]{0:T(1024)(128)(2,1)}, u32[]{:S(2)}) copy-start(bf16[6144]{0:T(1024)(128)(2,1)} %param.15) | copy-start | bytes 36868
  10.2 6.2 %collective-permute-start = (bf16[2]{0:T(256)(128)(2,1)S(1)}, bf16[2]{0:T(256)(128)(2,1)S(1)}, u32[]{:S(2)}, u32[]{:S(2)}) collective-permute-start(bf16[2]{0:T(256)(128)(2,1)S(1)} %convert_element_type.46), channel_id=1, source_target_pairs={{0,8},{1,9},{2,10},{3,11},{4,12},{5,13},{6,14},{7,15},{8,0},{9,1},... | collective-permute-start | bytes 20 | tf_op jit(solution)/shard_map/ppermute | solution.py:15
  13.1 4.0 %collective-permute-start.1 = (bf16[2,6144]{1,0:T(2,128)(2,1)S(1)}, bf16[2,6144]{1,0:T(2,128)(2,1)S(1)}, u32[]{:S(2)}, u32[]{:S(2)}) collective-permute-start(bf16[2,6144]{1,0:T(2,128)(2,1)S(1)} %gather_fusion.1), channel_id=1, source_target_pairs={{0,8},{1,9},{2,10},{3,11},{4,12},{5,13},{6,14},{7,15},{8,0},{9,1},... | collective-permute-start | bytes 73736 | tf_op jit(solution)/shard_map/ppermute | solution.py:15
  13.8 19.5 %collective-permute-start.2 = (bf16[2,48,2048]{2,1,0:T(8,128)(2,1)S(1)}, bf16[2,48,2048]{2,1,0:T(8,128)(2,1)S(1)}, u32[]{:S(2)}, u32[]{:S(2)}) collective-permute-start(bf16[2,48,2048]{2,1,0:T(8,128)(2,1)S(1)} %gather_fusion.2), channel_id=1, source_target_pairs={{0,8},{1,9},{2,10},{3,11},{4,12},{5,13},{6,14},{7,15},{8,0},{9,1},... | collective-permute-start | bytes 1179656 | tf_op jit(solution)/shard_map/ppermute | solution.py:15
  110.2 41.6 %all-to-all-start = ((bf16[16,6,6144]{2,1,0:T(8,128)(2,1)}), bf16[16,6,6144]{2,1,0:T(8,128)(2,1)S(1)}, u32[]{:S(2)}, u32[]{:S(2)}) async-start(bf16[16,6,6144]{2,1,0:T(8,128)(2,1)} %reshape.125), calls=%async_computation | async-start | bytes 3145728 | tf_op jit(solution)/shard_map/all_to_all | solution.py:87
Sparse Core Ops, SparseCore 0:
  37.3 42.8 all-gather.1
where the time goes:
time: 161 us; the launch traced here: 160 us
  waiting for transfers between devices  93.8 us (58%)
  matrix products  21 us (13%)
  local copies, waits for them, and re-layouts  20 us (12%)
  between operations  13.6 us (8%)
  starting transfers between devices  10.2 us (6%)
  other arithmetic  1.79 us (1%)
    all_gather x1, waiting for transfers between devices, body(): lax.all_gather(dispatch[None], 'attn', axis=0, tiled=True)  43 us
    all_to_all x1, waiting for transfers between devices, body(): lax.all_to_all(partials, 'attn', split_axis=0, concat_axis=0, tiled=True)  35.2 us
    ppermute x3, waiting for transfers between devices, partner(): lax.ppermute(array, axis, [(i, i ^ 1 << distance) for i in range(lax.axis...  15.5 us
    dot_general x1, matrix products, body(): jnp.dot(hidden, down_proj, preferred_element_type=jnp.float32)  12.4 us
    dynamic_slice x1, local copies, waits for them, and re-layouts, body(): lax.dynamic_index_in_dim(lax.all_gather(dispatch[None], 'attn', axis=0, t...  8.85 us
    dot_general x1, matrix products, body(): gated = jnp.dot(flat, gate_proj, preferred_element_type=jnp.float32)  6.73 us
    all_to_all x1, starting transfers between devices, body(): lax.all_to_all(partials, 'attn', split_axis=0, concat_axis=0, tiled=True)  5.42 us
    ppermute x3, starting transfers between devices, partner(): lax.ppermute(array, axis, [(i, i ^ 1 << distance) for i in range(lax.axis...  4.82 us
  transfers between devices with their start and end apart: 5, of which 3 were waited for; matrix products, arithmetic and copies ran while one was open for 2% of the time, Pallas kernels for 0%

commit v1 on v0

--- a/solution.py
+++ b/solution.py
@@ -1,6 +1,9 @@
+import functools
 import jax
 import jax.numpy as jnp
 from jax import lax
+from jax.experimental import pallas as pl
+from jax.experimental.pallas import tpu as pltpu
 from jax.sharding import PartitionSpec as P
 
 HQ = 48
@@ -9,6 +12,403 @@
 EXPERTS = 2
 LMAX = 48
 CAP = 6
+GROUP = HQ // KVH
+MESH = pl.DeviceIdType.MESH
+F32 = jnp.float32
+BF16 = jnp.bfloat16
+RANKS = 16
+ROWS = 8
+PIECES = 4
+COLS = 1024
+
+
+def layer_kernel(
+    lengths, handoff, routes, q_ref, gain_ref, router_ref, kv_hbm, wg_hbm, wu_hbm, wd_hbm, out_ref,
+    kv, wg, wu, wd, gathered, x, hidden, codes_out, codes, part, from_core, sum_core, from_first,
+    sum_first, from_second, own_sum, sum_second, from_partner, own_rows, own_gate,
+    kv_sem, w_sem, code_send, code_recv, g_send, g_recv, r_send, r_recv,
+):
+    me = lax.axis_index("attn")
+    z, y, core = me // 4, (me // 2) % 2, me % 2
+    zp, zh = z % 2, z // 2
+    sibling, across = me + 1 - 2 * core, me + 2 - 4 * y
+    beside = me + 4 - 8 * zp
+    partner = me + 8 - 16 * zh
+    width = q_ref.shape[1]
+    half = width // 2
+    chunks = width // COLS
+
+    def remote(src, dst, send, recv, to):
+        return pltpu.make_async_remote_copy(
+            src_ref=src, dst_ref=dst, send_sem=send, recv_sem=recv,
+            device_id={"attn": to}, device_id_type=MESH,
+        )
+
+    barrier = pltpu.get_barrier_semaphore()
+
+    def greet(step, carry):
+        pl.semaphore_signal(
+            barrier, inc=1, device_id={"attn": (me + step) % RANKS}, device_id_type=MESH
+        )
+        return carry
+
+    lax.fori_loop(1, RANKS, greet, 0)
+
+    kv_copy = pltpu.make_async_copy(kv_hbm, kv, kv_sem)
+    kv_copy.start()
+    loads = []
+    for index, (src, dst) in enumerate(((wg_hbm, wg), (wu_hbm, wu), (wd_hbm, wd))):
+        size = dst.shape[0] // PIECES
+        for piece in range(PIECES):
+            rows = pl.ds(piece * size, size)
+            loads.append(pltpu.make_async_copy(src.at[rows], dst.at[rows], w_sem.at[index, piece]))
+            loads[-1].start()
+
+    h0, h1 = handoff[0, 0], handoff[0, 1]
+    low, high = jnp.minimum(h0, h1), jnp.maximum(h0, h1)
+
+    def order_of(shape):
+        row = lax.broadcasted_iota(jnp.int32, shape, 0)
+        kept = row + (row >= low).astype(jnp.int32)
+        kept = kept + (kept >= high).astype(jnp.int32)
+        return jnp.where(row == 6, h0, jnp.where(row == 7, h1, kept))
+
+    slot = lax.broadcasted_iota(jnp.int32, (ROWS, 128), 0)
+    place = slot - (slot > h0).astype(jnp.int32) - (slot > h1).astype(jnp.int32)
+    source = jnp.where(
+        slot == h0, partner * ROWS + 6, jnp.where(slot == h1, partner * ROWS + 7, me * ROWS + place)
+    )
+    route = jnp.zeros((ROWS, 128), jnp.int32)
+    for t in range(ROWS):
+        route = jnp.where(slot == t, routes[t, 0], route)
+    for e in range(EXPERTS):
+        codes_out[e] = jnp.where(route == e, source, -1)
+    spot = core * 8 + y * 4 + zp * 2 + zh
+
+    order = order_of((ROWS, ROWS))
+    pick = (lax.broadcasted_iota(jnp.int32, (ROWS, ROWS), 1) == order).astype(BF16)
+    queries = jnp.dot(pick, q_ref[...], preferred_element_type=F32)
+    span = (ROWS, ROWS * LMAX)
+    column = lax.broadcasted_iota(jnp.int32, span, 1)
+    holder = jnp.zeros(span, jnp.int32)
+    for t in range(1, ROWS):
+        holder = holder + (column >= t * LMAX).astype(jnp.int32)
+    position = column - holder * LMAX
+    wide = order_of(span)
+    limit = jnp.zeros(span, jnp.int32)
+    for t in range(ROWS):
+        limit = jnp.where(wide == t, lengths[t], limit)
+    visible = jnp.where((holder == wide) & (position < limit), 0.0, -jnp.inf).astype(F32)
+    visible = jnp.concatenate([visible] * GROUP, axis=0)
+    kv_copy.wait()
+
+    def head(k):
+        begin = k * GROUP * HD
+        rows = jnp.concatenate(
+            [queries[:, begin + g * HD:begin + (g + 1) * HD] for g in range(GROUP)], axis=0
+        ).astype(BF16)
+        keys = kv[:, :, k * HD:(k + 1) * HD].reshape(ROWS * LMAX, HD)
+        values = kv[:, :, (KVH + k) * HD:(KVH + k + 1) * HD].reshape(ROWS * LMAX, HD)
+        scores = lax.dot_general(
+            rows, keys, (((1,), (1,)), ((), ())), preferred_element_type=F32
+        ) * HD ** (-0.5) + visible
+        weights = jnp.exp(scores - jnp.max(scores, axis=-1, keepdims=True))
+        weights = (weights / jnp.sum(weights, axis=-1, keepdims=True)).astype(BF16)
+        return jnp.dot(weights, values, preferred_element_type=F32)
+
+    for k in range(KVH // 2):
+        left, right = head(k), head(k + KVH // 2)
+        for g in range(GROUP):
+            rows = slice(g * ROWS, (g + 1) * ROWS)
+            at = (k * GROUP + g) * HD
+            gathered[me, :, at:at + HD] = jnp.concatenate([left[rows], right[rows]], axis=0).astype(BF16)
+
+    pl.semaphore_wait(barrier, RANKS - 1)
+
+    UP, DOWN, ACROSS, CORE = range(4)
+
+    def send(kind, block, to):
+        return remote(
+            gathered.at[block], gathered.at[block], g_send.at[kind, block], g_recv.at[block], to
+        )
+
+    def arrived(block):
+        send(CORE, block, sibling).wait_recv()
+
+    def code_copy(step):
+        to = (me + step) % RANKS
+        return remote(
+            codes_out.at[to // 8], codes.at[spot], code_send.at[step], code_recv.at[spot], to
+        )
+
+    def spread(finish):
+        def act(copy):
+            copy.wait_send() if finish else copy.start()
+
+        def first(block):
+            act(send(ACROSS, block, across))
+            act(send(CORE, block, sibling))
+
+        pl.when(z < 3)(lambda: act(send(UP, me, me + 4)))
+        pl.when(z > 0)(lambda: act(send(DOWN, me, me - 4)))
+        first(me)
+
+        def codes_step(step, carry):
+            act(code_copy(step))
+            return carry
+
+        lax.fori_loop(1, RANKS, codes_step, 0)
+
+        def from_below(far):
+            block = me - 4 * far
+            if not finish:
+                arrived(block)
+            pl.when(z < 3)(lambda: act(send(UP, block, me + 4)))
+            first(block)
+
+        def from_above(far):
+            block = me + 4 * far
+            if not finish:
+                arrived(block)
+            pl.when(z > 0)(lambda: act(send(DOWN, block, me - 4)))
+            first(block)
+
+        def hand_on(block):
+            if not finish:
+                arrived(block)
+            act(send(CORE, block, sibling))
+
+        for far in range(1, 5):
+            if far < 4:
+                pl.when(z >= far)(functools.partial(from_below, far))
+                pl.when(z + far < 4)(functools.partial(from_above, far))
+            if far == 1:
+                hand_on(across)
+            else:
+                pl.when(z >= far - 1)(functools.partial(hand_on, across - 4 * (far - 1)))
+                pl.when(z + far - 1 < 4)(functools.partial(hand_on, across + 4 * (far - 1)))
+
+    spread(False)
+    codes[spot] = codes_out[me // 8]
+
+    def code_wait(step, carry):
+        other = (me + step) % RANKS
+        there = (other % 2) * 8 + ((other // 2) % 2) * 4 + ((other // 4) % 2) * 2 + other // 8
+        remote(
+            codes.at[there], codes.at[there], code_send.at[step], code_recv.at[there], sibling
+        ).wait_recv()
+        return carry
+
+    lax.fori_loop(1, RANKS, code_wait, 0)
+
+    def sibling_wait(chip, carry):
+        arrived(chip * 2 + 1 - core)
+        return carry
+
+    lax.fori_loop(0, RANKS // 2, sibling_wait, 0)
+
+    def halves(first, second):
+        return (
+            jnp.concatenate([first[:ROWS], second[:ROWS]], axis=0),
+            jnp.concatenate([first[ROWS:], second[ROWS:]], axis=0),
+        )
+
+    def norm(left, right):
+        total = jnp.sum(left * left, axis=-1, keepdims=True) + jnp.sum(
+            right * right, axis=-1, keepdims=True
+        )
+        scale = lax.rsqrt(total / width + 1e-05)
+        return (
+            (left * scale * gain_ref[:, :half].astype(F32)).astype(BF16),
+            (right * scale * gain_ref[:, half:].astype(F32)).astype(BF16),
+        )
+
+    def norm_step(chip, carry):
+        left, right = halves(gathered[2 * chip].astype(F32), gathered[2 * chip + 1].astype(F32))
+        left, right = norm(left, right)
+        rows = pl.ds(pl.multiple_of(chip * 16, 16), 16)
+        x[rows, :half] = left
+        x[rows, half:] = right
+        return carry
+
+    lax.fori_loop(0, RANKS // 2, norm_step, 0)
+
+    for copy in loads[:2 * PIECES]:
+        copy.wait()
+
+    def up_step(tile, carry):
+        columns = pl.ds(pl.multiple_of(tile * 256, 256), 256)
+        gated = jnp.dot(x[...], wg[:, columns], preferred_element_type=F32)
+        upward = jnp.dot(x[...], wu[:, columns], preferred_element_type=F32)
+        hidden[:, columns] = (gated / (1.0 + jnp.exp(-gated)) * upward).astype(BF16)
+        return carry
+
+    lax.fori_loop(0, wg.shape[1] // 256, up_step, 0)
+
+    chosen = codes[...].reshape(RANKS * ROWS, 128)
+    select = (lax.broadcasted_iota(jnp.int32, chosen.shape, 1) == chosen).astype(BF16)
+    hidden[...] = jnp.dot(select, hidden[...], preferred_element_type=F32).astype(BF16)
+    for copy in loads[2 * PIECES:]:
+        copy.wait()
+
+    def core_copy(j):
+        return remote(
+            part.at[j, 1 - core], from_core.at[j], r_send.at[0, j], r_recv.at[0, j], sibling
+        )
+
+    def first_copy(j):
+        if j % 2 == 0:
+            return remote(
+                sum_core.at[j, 1 - y], from_first.at[j], r_send.at[1, j], r_recv.at[1, j], across
+            )
+        return remote(
+            sum_core.at[j, :, 1 - zp], from_first.at[j], r_send.at[1, j], r_recv.at[1, j], beside
+        )
+
+    def second_copy(j):
+        if j % 2 == 0:
+            return remote(
+                sum_first.at[j, 1 - zp], from_second.at[j], r_send.at[2, j], r_recv.at[2, j], beside
+            )
+        return remote(
+            sum_first.at[j, 1 - y], from_second.at[j], r_send.at[2, j], r_recv.at[2, j], across
+        )
+
+    def partner_copy(j):
+        return remote(
+            sum_second.at[j], from_partner.at[j], r_send.at[3, j], r_recv.at[3, j], partner
+        )
+
+    def down(j):
+        part[j] = jnp.dot(
+            hidden[...], wd[:, j * COLS:(j + 1) * COLS], preferred_element_type=F32
+        ).astype(BF16).reshape(2, 2, 2, 16, COLS)
+        core_copy(j).start()
+
+    def add_core(j):
+        core_copy(j).wait_recv()
+        sum_core[j] = (part[j, core].astype(F32) + from_core[j].astype(F32)).astype(BF16)
+        first_copy(j).start()
+
+    def add_first(j):
+        first_copy(j).wait_recv()
+        mine = sum_core[j, y] if j % 2 == 0 else sum_core[j, :, zp]
+        sum_first[j] = (mine.astype(F32) + from_first[j].astype(F32)).astype(BF16)
+        second_copy(j).start()
+
+    def add_second(j):
+        second_copy(j).wait_recv()
+        mine = sum_first[j, zp] if j % 2 == 0 else sum_first[j, y]
+        total = mine.astype(F32) + from_second[j].astype(F32)
+        upper = zh == 1
+        own_sum[j] = jnp.where(upper, total[ROWS:], total[:ROWS])
+        other = jnp.where(upper, total[:ROWS], total[ROWS:])
+        sum_second[j] = jnp.concatenate(
+            [other[:, :COLS // 2], other[:, COLS // 2:]], axis=0
+        ).astype(BF16)
+        partner_copy(j).start()
+
+    def own():
+        near = jnp.where(
+            slot == h0, ROWS + 6, jnp.where(slot == h1, ROWS + 7, place)
+        )[:, :2 * ROWS]
+        take = (lax.broadcasted_iota(jnp.int32, near.shape, 1) == near).astype(BF16)
+        left, right = halves(gathered[me].astype(F32), gathered[partner].astype(F32))
+        left = jnp.dot(take, left.astype(BF16), preferred_element_type=F32)
+        right = jnp.dot(take, right.astype(BF16), preferred_element_type=F32)
+        own_rows[:, :half] = left
+        own_rows[:, half:] = right
+        left, right = norm(left, right)
+        logits = []
+        for e in range(EXPERTS):
+            weight = router_ref[e:e + 1, :].astype(F32)
+            logits.append(
+                jnp.sum(left.astype(F32) * weight[:, :half], axis=-1, keepdims=True)
+                + jnp.sum(right.astype(F32) * weight[:, half:], axis=-1, keepdims=True)
+            )
+        chosen_logit = jnp.where(route[:, :1] == 0, logits[0], logits[1])
+        odds = jnp.exp(logits[0] - chosen_logit) + jnp.exp(logits[1] - chosen_logit)
+        own_gate[...] = jnp.broadcast_to(1.0 / odds, own_gate.shape)
+
+    def finish(j):
+        partner_copy(j).wait_recv()
+        other = from_partner[j].astype(F32)
+        other = jnp.concatenate([other[:ROWS], other[ROWS:]], axis=1)
+        columns = slice(j * COLS, (j + 1) * COLS)
+        out_ref[:, columns] = (
+            own_rows[:, columns] + own_gate[:, :1] * (own_sum[j] + other)
+        ).astype(BF16)
+
+    for step in range(chunks + 4):
+        if step < chunks:
+            down(step)
+        if step == 1:
+            own()
+        for late, act in enumerate((add_core, add_first, add_second, finish)):
+            if 0 <= step - late - 1 < chunks:
+                act(step - late - 1)
+
+    spread(True)
+    for j in range(chunks):
+        for copy in (core_copy, first_copy, second_copy, partner_copy):
+            copy(j).wait_send()
+
+
+def fused(queries, kv_cache, lengths, handoff, routes, norm_gain, router, gate_proj, up_proj, down_proj):
+    width = queries.shape[1]
+    inner = gate_proj.shape[1]
+    chunks = width // COLS
+    smem = pl.BlockSpec(memory_space=pltpu.SMEM)
+    vmem = pl.BlockSpec(memory_space=pltpu.VMEM)
+    hbm = pl.BlockSpec(memory_space=pl.ANY)
+    dma = pltpu.SemaphoreType.DMA
+    return pl.pallas_call(
+        layer_kernel,
+        out_shape=jax.ShapeDtypeStruct(queries.shape, BF16),
+        in_specs=[smem, smem, smem, vmem, vmem, vmem, hbm, hbm, hbm, hbm],
+        out_specs=vmem,
+        scratch_shapes=[
+            pltpu.VMEM(kv_cache.shape, BF16),
+            pltpu.VMEM(gate_proj.shape, BF16),
+            pltpu.VMEM(up_proj.shape, BF16),
+            pltpu.VMEM(down_proj.shape, BF16),
+            pltpu.VMEM((RANKS, 2 * ROWS, width // 2), BF16),
+            pltpu.VMEM((RANKS * ROWS, width), BF16),
+            pltpu.VMEM((RANKS * ROWS, inner), BF16),
+            pltpu.VMEM((EXPERTS, ROWS, 128), jnp.int32),
+            pltpu.VMEM((RANKS, ROWS, 128), jnp.int32),
+            pltpu.VMEM((chunks, 2, 2, 2, 16, COLS), BF16),
+            pltpu.VMEM((chunks, 2, 2, 16, COLS), BF16),
+            pltpu.VMEM((chunks, 2, 2, 16, COLS), BF16),
+            pltpu.VMEM((chunks, 2, 16, COLS), BF16),
+            pltpu.VMEM((chunks, 2, 16, COLS), BF16),
+            pltpu.VMEM((chunks, 16, COLS), BF16),
+            pltpu.VMEM((chunks, ROWS, COLS), F32),
+            pltpu.VMEM((chunks, 16, COLS // 2), BF16),
+            pltpu.VMEM((chunks, 16, COLS // 2), BF16),
+            pltpu.VMEM((ROWS, width), F32),
+            pltpu.VMEM((ROWS, 128), F32),
+            dma,
+            dma((3, PIECES)),
+            dma((RANKS,)),
+            dma((RANKS,)),
+            dma((4, RANKS)),
+            dma((RANKS,)),
+            dma((4, chunks)),
+            dma((4, chunks)),
+        ],
+        compiler_params=pltpu.CompilerParams(
+            collective_id=0, has_side_effects=True, vmem_limit_bytes=60 * 1024 * 1024
+        ),
+        cost_estimate=pl.CostEstimate(
+            flops=6 * RANKS * ROWS * width * inner,
+            bytes_accessed=6 * width * inner,
+            transcendentals=0,
+        ),
+    )(
+        lengths, handoff, routes, queries, norm_gain[None, :], router.T, kv_cache,
+        gate_proj, up_proj, down_proj,
+    )
 
 
 def partner(array, axis, distance):
@@ -39,16 +439,15 @@
     queries, kv_cache, lengths, handoff, routes, norm_gain, router, gate_proj, up_proj, down_proj
 ):
     ranks = lax.axis_size("attn")
+    if ranks == RANKS and queries.shape[0] == ROWS:
+        return fused(
+            queries, kv_cache, lengths, handoff, routes, norm_gain, router,
+            gate_proj, up_proj, down_proj,
+        )
     picks = handoff[0]
     highest_bit = ranks.bit_length() - 2
-    moved = partner(
-        (queries[picks], kv_cache[picks], lengths[picks].astype(jnp.bfloat16)), "attn", highest_bit
-    )
-    attended = attend(
-        queries.at[picks].set(moved[0]),
-        kv_cache.at[picks].set(moved[1]),
-        lengths.at[picks].set(moved[2].astype(jnp.int32)),
-    )
+    attended = attend(queries, kv_cache, lengths)
+    attended = attended.at[picks].set(partner(attended[picks], "attn", highest_bit))
     attended_f = attended.astype(jnp.float32)
     scale_rows = lax.rsqrt(jnp.mean(attended_f * attended_f, axis=-1, keepdims=True) + 1e-05)
     normed = (attended_f * scale_rows * norm_gain.astype(jnp.float32)).astype(jnp.bfloat16)

time: 161 us -> 69.4 us (0.43)
  the two profiles are of different devices: /device:TPU:13 before, /device:TPU:0 now
where the time goes in v1:
time: 69.4 us; the launch traced here: 69.2 us
  Pallas kernels  65 us (94%)
  local copies, waits for them, and re-layouts  4.19 us (6%)
    pallas_call x1, Pallas kernels, fused(): pl.pallas_call(layer_kernel, out_shape=jax.ShapeDtypeStruct(queries.shape...  65 us
    unnamed x2, local copies, waits for them, and re-layouts  2.86 us

profile of v1, /device:TPU:0, one launch (start us, length us, event | category | flops | bytes accessed | tf_op | source)
XLA Modules:
  0.0 69.2 jit_solution(15662096035005641297)
XLA Ops:
  0.0 1.3 %copy.11.routes = s32[8,1]{1,0:T(8,128)} copy(s32[8,1]{0,1:T(1,128)} %param.14) | data formatting | bytes 64 | tf_op args[4]
  1.3 1.3 %broadcast_in_dim.3.gain_ref = bf16[1,6144]{1,0:T(2,128)(2,1)} reshape(bf16[6144]{0:T(1024)(128)(2,1)} %param.15) | data formatting | bytes 24576 | tf_op jit(solution)/shard_map/broadcast_in_dim | solution.py:409
  2.7 65.0 %shard_map.100 = bf16[8,6144]{1,0:T(8,128)(2,1)} custom-call(s32[8]{0:T(128)} %lengths.1, s32[1,2]{1,0:T(1,128)} %handoff.1, s32[8,1]{1,0:T(8,128)} %copy.11.routes, bf16[8,6144]{1,0:T(8,128)(2,1)} %q_ref.1, bf16[1,6144]{1,0:T(2,128)(2,1)} %broadcast_in_dim.3.gain_ref, bf16[2,6144]{1,0:T(2,128)(2,1)} %bitcast.1, bf16[8,48,2048]{2,1,0:T(8,128)(2,1)} %kv_hbm.1, ...), custom_call_target="tpu_custom_call" | custom-call | flops 4831838208 | bytes 37748736 | tf_op jit(solution)/shard_map/pallas_call | solution.py:365
  67.7 1.5 %copy.13 = bf16[8,6144]{1,0:T(8,128)(2,1)} copy(bf16[8,6144]{1,0:T(8,128)(2,1)} %shard_map.100) | data formatting | bytes 196608

commit v2 on v1

--- a/solution.py
+++ b/solution.py
@@ -18,15 +18,18 @@
 BF16 = jnp.bfloat16
 RANKS = 16
 ROWS = 8
-PIECES = 4
+PIECES = 8
+FIRST = 8
+EACH = 2
+LAGS = (2, 5, 8, 11)
 COLS = 1024
 
 
 def layer_kernel(
     lengths, handoff, routes, q_ref, gain_ref, router_ref, kv_hbm, wg_hbm, wu_hbm, wd_hbm, out_ref,
-    kv, wg, wu, wd, gathered, x, hidden, codes_out, codes, part, from_core, sum_core, from_first,
+    kv, wg, wu, wd, gathered, x, hidden, part, from_core, sum_core, from_first,
     sum_first, from_second, own_sum, sum_second, from_partner, own_rows, own_gate,
-    kv_sem, w_sem, code_send, code_recv, g_send, g_recv, r_send, r_recv,
+    kv_sem, w_sem, g_send, g_recv, r_send, r_recv,
 ):
     me = lax.axis_index("attn")
     z, y, core = me // 4, (me // 2) % 2, me % 2
@@ -46,13 +49,13 @@
 
     barrier = pltpu.get_barrier_semaphore()
 
-    def greet(step, carry):
-        pl.semaphore_signal(
-            barrier, inc=1, device_id={"attn": (me + step) % RANKS}, device_id_type=MESH
-        )
-        return carry
-
-    lax.fori_loop(1, RANKS, greet, 0)
+    def greet(to):
+        pl.semaphore_signal(barrier, inc=1, device_id={"attn": to}, device_id_type=MESH)
+
+    pl.when(z < 3)(lambda: greet(me + 4))
+    pl.when(z > 0)(lambda: greet(me - 4))
+    for to in (across, sibling, partner):
+        greet(to)
 
     kv_copy = pltpu.make_async_copy(kv_hbm, kv, kv_sem)
     kv_copy.start()
@@ -62,7 +65,15 @@
         for piece in range(PIECES):
             rows = pl.ds(piece * size, size)
             loads.append(pltpu.make_async_copy(src.at[rows], dst.at[rows], w_sem.at[index, piece]))
-            loads[-1].start()
+
+    started = [0]
+
+    def load(amount):
+        for copy in loads[started[0]:started[0] + amount]:
+            copy.start()
+        started[0] += amount
+
+    load(FIRST)
 
     h0, h1 = handoff[0, 0], handoff[0, 1]
     low, high = jnp.minimum(h0, h1), jnp.maximum(h0, h1)
@@ -80,10 +91,10 @@
     )
     route = jnp.zeros((ROWS, 128), jnp.int32)
     for t in range(ROWS):
-        route = jnp.where(slot == t, routes[t, 0], route)
-    for e in range(EXPERTS):
-        codes_out[e] = jnp.where(route == e, source, -1)
-    spot = core * 8 + y * 4 + zp * 2 + zh
+        route = jnp.where(slot == t, routes[t], route)
+    gathered[me, :, half:] = jnp.concatenate(
+        [jnp.where(route == e, source, -1).astype(F32) for e in range(EXPERTS)], axis=0
+    ).astype(BF16)
 
     order = order_of((ROWS, ROWS))
     pick = (lax.broadcasted_iota(jnp.int32, (ROWS, ROWS), 1) == order).astype(BF16)
@@ -123,7 +134,7 @@
             at = (k * GROUP + g) * HD
             gathered[me, :, at:at + HD] = jnp.concatenate([left[rows], right[rows]], axis=0).astype(BF16)
 
-    pl.semaphore_wait(barrier, RANKS - 1)
+    pl.semaphore_wait(barrier, 3 + (z < 3).astype(jnp.int32) + (z > 0).astype(jnp.int32))
 
     UP, DOWN, ACROSS, CORE = range(4)
 
@@ -135,12 +146,6 @@
     def arrived(block):
         send(CORE, block, sibling).wait_recv()
 
-    def code_copy(step):
-        to = (me + step) % RANKS
-        return remote(
-            codes_out.at[to // 8], codes.at[spot], code_send.at[step], code_recv.at[spot], to
-        )
-
     def spread(finish):
         def act(copy):
             copy.wait_send() if finish else copy.start()
@@ -152,12 +157,6 @@
         pl.when(z < 3)(lambda: act(send(UP, me, me + 4)))
         pl.when(z > 0)(lambda: act(send(DOWN, me, me - 4)))
         first(me)
-
-        def codes_step(step, carry):
-            act(code_copy(step))
-            return carry
-
-        lax.fori_loop(1, RANKS, codes_step, 0)
 
         def from_below(far):
             block = me - 4 * far
@@ -179,6 +178,8 @@
             act(send(CORE, block, sibling))
 
         for far in range(1, 5):
+            if not finish:
+                load(EACH)
             if far < 4:
                 pl.when(z >= far)(functools.partial(from_below, far))
                 pl.when(z + far < 4)(functools.partial(from_above, far))
@@ -189,23 +190,13 @@
                 pl.when(z + far - 1 < 4)(functools.partial(hand_on, across + 4 * (far - 1)))
 
     spread(False)
-    codes[spot] = codes_out[me // 8]
-
-    def code_wait(step, carry):
-        other = (me + step) % RANKS
-        there = (other % 2) * 8 + ((other // 2) % 2) * 4 + ((other // 4) % 2) * 2 + other // 8
-        remote(
-            codes.at[there], codes.at[there], code_send.at[step], code_recv.at[there], sibling
-        ).wait_recv()
-        return carry
-
-    lax.fori_loop(1, RANKS, code_wait, 0)
-
     def sibling_wait(chip, carry):
         arrived(chip * 2 + 1 - core)
         return carry
 
     lax.fori_loop(0, RANKS // 2, sibling_wait, 0)
+
+    load(len(loads) - started[0])
 
     def halves(first, second):
         return (
@@ -219,12 +210,12 @@
         )
         scale = lax.rsqrt(total / width + 1e-05)
         return (
-            (left * scale * gain_ref[:, :half].astype(F32)).astype(BF16),
-            (right * scale * gain_ref[:, half:].astype(F32)).astype(BF16),
+            (left * scale * gain_ref[pl.ds(0, half)].astype(F32)[None, :]).astype(BF16),
+            (right * scale * gain_ref[pl.ds(half, half)].astype(F32)[None, :]).astype(BF16),
         )
 
     def norm_step(chip, carry):
-        left, right = halves(gathered[2 * chip].astype(F32), gathered[2 * chip + 1].astype(F32))
+        left, right = halves(gathered[2 * chip, :, :half].astype(F32), gathered[2 * chip + 1, :, :half].astype(F32))
         left, right = norm(left, right)
         rows = pl.ds(pl.multiple_of(chip * 16, 16), 16)
         x[rows, :half] = left
@@ -245,8 +236,14 @@
 
     lax.fori_loop(0, wg.shape[1] // 256, up_step, 0)
 
-    chosen = codes[...].reshape(RANKS * ROWS, 128)
-    select = (lax.broadcasted_iota(jnp.int32, chosen.shape, 1) == chosen).astype(BF16)
+    chosen = []
+    for spot in range(RANKS):
+        rank = (spot % 2 * 2 + spot // 2 % 2) * 4 + spot // 4 % 2 * 2 + spot // 8
+        codes = gathered[rank, :, half:].astype(F32)
+        chosen.append(jnp.where(zh == 0, codes[:ROWS], codes[ROWS:]))
+    chosen = jnp.concatenate(chosen, axis=0)
+    lane = lax.broadcasted_iota(jnp.int32, chosen.shape, 1).astype(F32)
+    select = (lane == chosen).astype(BF16)
     hidden[...] = jnp.dot(select, hidden[...], preferred_element_type=F32).astype(BF16)
     for copy in loads[2 * PIECES:]:
         copy.wait()
@@ -313,7 +310,7 @@
             slot == h0, ROWS + 6, jnp.where(slot == h1, ROWS + 7, place)
         )[:, :2 * ROWS]
         take = (lax.broadcasted_iota(jnp.int32, near.shape, 1) == near).astype(BF16)
-        left, right = halves(gathered[me].astype(F32), gathered[partner].astype(F32))
+        left, right = halves(gathered[me, :, :half].astype(F32), gathered[partner, :, :half].astype(F32))
         left = jnp.dot(take, left.astype(BF16), preferred_element_type=F32)
         right = jnp.dot(take, right.astype(BF16), preferred_element_type=F32)
         own_rows[:, :half] = left
@@ -339,14 +336,14 @@
             own_rows[:, columns] + own_gate[:, :1] * (own_sum[j] + other)
         ).astype(BF16)
 
-    for step in range(chunks + 4):
+    for step in range(chunks + LAGS[-1]):
         if step < chunks:
             down(step)
-        if step == 1:
+        if step == chunks - 1:
             own()
-        for late, act in enumerate((add_core, add_first, add_second, finish)):
-            if 0 <= step - late - 1 < chunks:
-                act(step - late - 1)
+        for late, act in zip(LAGS, (add_core, add_first, add_second, finish)):
+            if 0 <= step - late < chunks:
+                act(step - late)
 
     spread(True)
     for j in range(chunks):
@@ -372,11 +369,9 @@
             pltpu.VMEM(gate_proj.shape, BF16),
             pltpu.VMEM(up_proj.shape, BF16),
             pltpu.VMEM(down_proj.shape, BF16),
-            pltpu.VMEM((RANKS, 2 * ROWS, width // 2), BF16),
+            pltpu.VMEM((RANKS, 2 * ROWS, width // 2 + 128), BF16),
             pltpu.VMEM((RANKS * ROWS, width), BF16),
             pltpu.VMEM((RANKS * ROWS, inner), BF16),
-            pltpu.VMEM((EXPERTS, ROWS, 128), jnp.int32),
-            pltpu.VMEM((RANKS, ROWS, 128), jnp.int32),
             pltpu.VMEM((chunks, 2, 2, 2, 16, COLS), BF16),
             pltpu.VMEM((chunks, 2, 2, 16, COLS), BF16),
             pltpu.VMEM((chunks, 2, 2, 16, COLS), BF16),
@@ -390,8 +385,6 @@
             pltpu.VMEM((ROWS, 128), F32),
             dma,
             dma((3, PIECES)),
-            dma((RANKS,)),
-            dma((RANKS,)),
             dma((4, RANKS)),
             dma((RANKS,)),
             dma((4, chunks)),
@@ -406,7 +399,7 @@
             transcendentals=0,
         ),
     )(
-        lengths, handoff, routes, queries, norm_gain[None, :], router.T, kv_cache,
+        lengths, handoff, routes[:, 0], queries, norm_gain, router.T, kv_cache,
         gate_proj, up_proj, down_proj,
     )
 

time: 69.4 us -> 54.2 us (0.78)
  Pallas kernels: 65 us -> 52.5 us
  local copies, waits for them, and re-layouts: 4.19 us -> 1.54 us
    pallas_call x1, Pallas kernels: 65 us -> 52.5 us  [fused(): pl.pallas_call(layer_kernel, out_shape=jax.ShapeDtypeStruct(queries.shape...]
    broadcast_in_dim x1 -> x0, local copies, waits for them, and re-layouts: 1.33 us -> none  [fused(): norm_gain[None, :]]
    unnamed x2 -> x1, local copies, waits for them, and re-layouts: 2.86 us -> 1.54 us
where the time goes in v2:
time: 54.2 us; the launch traced here: 54 us
  Pallas kernels  52.5 us (97%)
  local copies, waits for them, and re-layouts  1.54 us (3%)
    pallas_call x1, Pallas kernels, fused(): pl.pallas_call(layer_kernel, out_shape=jax.ShapeDtypeStruct(queries.shape...  52.5 us
    unnamed x1, local copies, waits for them, and re-layouts  1.54 us

profile of v2, /device:TPU:0, one launch (start us, length us, event | category | flops | bytes accessed | tf_op | source)
XLA Modules:
  0.0 54.0 jit_solution(1257570513659197638)
XLA Ops:
  0.0 52.5 %shard_map.100 = bf16[8,6144]{1,0:T(8,128)(2,1)} custom-call(s32[8]{0:T(128)} %lengths.1, s32[1,2]{1,0:T(1,128)} %handoff.1, s32[8]{0:T(128)} %bitcast.3, bf16[8,6144]{1,0:T(8,128)(2,1)} %q_ref.1, bf16[6144]{0:T(1024)(128)(2,1)} %gain_ref.1, bf16[2,6144]{1,0:T(2,128)(2,1)} %bitcast.2, bf16[8,48,2048]{2,1,0:T(8,128)(2,1)} %kv_hbm.1, ...), custom_call_target="tpu_custom_call" | custom-call | flops 4831838208 | bytes 37748736 | tf_op jit(solution)/shard_map/pallas_call | solution.py:362
  52.5 1.5 %copy.12 = bf16[8,6144]{1,0:T(8,128)(2,1)} copy(bf16[8,6144]{1,0:T(8,128)(2,1)} %shard_map.100) | data formatting | bytes 196608

commit v3 on v2

--- a/solution.py
+++ b/solution.py
@@ -19,8 +19,8 @@
 RANKS = 16
 ROWS = 8
 PIECES = 8
-FIRST = 8
-EACH = 2
+FIRST = 24
+PARTS = 2
 LAGS = (2, 5, 8, 11)
 COLS = 1024
 
@@ -72,8 +72,6 @@
         for copy in loads[started[0]:started[0] + amount]:
             copy.start()
         started[0] += amount
-
-    load(FIRST)
 
     h0, h1 = handoff[0, 0], handoff[0, 1]
     low, high = jnp.minimum(h0, h1), jnp.maximum(h0, h1)
@@ -112,6 +110,7 @@
     visible = jnp.where((holder == wide) & (position < limit), 0.0, -jnp.inf).astype(F32)
     visible = jnp.concatenate([visible] * GROUP, axis=0)
     kv_copy.wait()
+    load(FIRST)
 
     def head(k):
         begin = k * GROUP * HD
@@ -138,60 +137,63 @@
 
     UP, DOWN, ACROSS, CORE = range(4)
 
-    def send(kind, block, to):
-        return remote(
-            gathered.at[block], gathered.at[block], g_send.at[kind, block], g_recv.at[block], to
-        )
-
-    def arrived(block):
-        send(CORE, block, sibling).wait_recv()
+    def send(kind, block, piece, to):
+        size = (half + 128) // 128 // PARTS * 128
+        begin = piece * size
+        size = size if piece < PARTS - 1 else half + 128 - begin
+        ref = gathered.at[block, :, pl.ds(begin, size)]
+        return remote(ref, ref, g_send.at[kind, block, piece], g_recv.at[block, piece], to)
+
+    def arrived(block, piece):
+        send(CORE, block, piece, sibling).wait_recv()
 
     def spread(finish):
         def act(copy):
             copy.wait_send() if finish else copy.start()
 
-        def first(block):
-            act(send(ACROSS, block, across))
-            act(send(CORE, block, sibling))
-
-        pl.when(z < 3)(lambda: act(send(UP, me, me + 4)))
-        pl.when(z > 0)(lambda: act(send(DOWN, me, me - 4)))
-        first(me)
-
-        def from_below(far):
+        def first(block, piece):
+            act(send(ACROSS, block, piece, across))
+            act(send(CORE, block, piece, sibling))
+
+        for piece in range(PARTS):
+            pl.when(z < 3)(lambda: act(send(UP, me, piece, me + 4)))
+            pl.when(z > 0)(lambda: act(send(DOWN, me, piece, me - 4)))
+            first(me, piece)
+
+        def from_below(far, piece):
             block = me - 4 * far
             if not finish:
-                arrived(block)
-            pl.when(z < 3)(lambda: act(send(UP, block, me + 4)))
-            first(block)
-
-        def from_above(far):
+                arrived(block, piece)
+            pl.when(z < 3)(lambda: act(send(UP, block, piece, me + 4)))
+            first(block, piece)
+
+        def from_above(far, piece):
             block = me + 4 * far
             if not finish:
-                arrived(block)
-            pl.when(z > 0)(lambda: act(send(DOWN, block, me - 4)))
-            first(block)
-
-        def hand_on(block):
+                arrived(block, piece)
+            pl.when(z > 0)(lambda: act(send(DOWN, block, piece, me - 4)))
+            first(block, piece)
+
+        def hand_on(block, piece):
             if not finish:
-                arrived(block)
-            act(send(CORE, block, sibling))
-
-        for far in range(1, 5):
-            if not finish:
-                load(EACH)
-            if far < 4:
-                pl.when(z >= far)(functools.partial(from_below, far))
-                pl.when(z + far < 4)(functools.partial(from_above, far))
-            if far == 1:
-                hand_on(across)
-            else:
-                pl.when(z >= far - 1)(functools.partial(hand_on, across - 4 * (far - 1)))
-                pl.when(z + far - 1 < 4)(functools.partial(hand_on, across + 4 * (far - 1)))
+                arrived(block, piece)
+            act(send(CORE, block, piece, sibling))
+
+        for far in range(1, 4):
+            for piece in range(PARTS):
+                pl.when(z >= far)(functools.partial(from_below, far, piece))
+                pl.when(z + far < 4)(functools.partial(from_above, far, piece))
+        for piece in range(PARTS):
+            hand_on(across, piece)
+        for far in range(1, 4):
+            for piece in range(PARTS):
+                pl.when(z >= far)(functools.partial(hand_on, across - 4 * far, piece))
+                pl.when(z + far < 4)(functools.partial(hand_on, across + 4 * far, piece))
 
     spread(False)
     def sibling_wait(chip, carry):
-        arrived(chip * 2 + 1 - core)
+        for piece in range(PARTS):
+            arrived(chip * 2 + 1 - core, piece)
         return carry
 
     lax.fori_loop(0, RANKS // 2, sibling_wait, 0)
@@ -254,7 +256,7 @@
         )
 
     def first_copy(j):
-        if j % 2 == 0:
+        if j % 3 != 2:
             return remote(
                 sum_core.at[j, 1 - y], from_first.at[j], r_send.at[1, j], r_recv.at[1, j], across
             )
@@ -263,7 +265,7 @@
         )
 
     def second_copy(j):
-        if j % 2 == 0:
+        if j % 3 != 2:
             return remote(
                 sum_first.at[j, 1 - zp], from_second.at[j], r_send.at[2, j], r_recv.at[2, j], beside
             )
@@ -289,13 +291,13 @@
 
     def add_first(j):
         first_copy(j).wait_recv()
-        mine = sum_core[j, y] if j % 2 == 0 else sum_core[j, :, zp]
+        mine = sum_core[j, y] if j % 3 != 2 else sum_core[j, :, zp]
         sum_first[j] = (mine.astype(F32) + from_first[j].astype(F32)).astype(BF16)
         second_copy(j).start()
 
     def add_second(j):
         second_copy(j).wait_recv()
-        mine = sum_first[j, zp] if j % 2 == 0 else sum_first[j, y]
+        mine = sum_first[j, zp] if j % 3 != 2 else sum_first[j, y]
         total = mine.astype(F32) + from_second[j].astype(F32)
         upper = zh == 1
         own_sum[j] = jnp.where(upper, total[ROWS:], total[:ROWS])
@@ -385,8 +387,8 @@
             pltpu.VMEM((ROWS, 128), F32),
             dma,
             dma((3, PIECES)),
-            dma((4, RANKS)),
-            dma((RANKS,)),
+            dma((4, RANKS, PARTS)),
+            dma((RANKS, PARTS)),
             dma((4, chunks)),
             dma((4, chunks)),
         ],

time: 54.2 us -> 49.7 us (0.917)
  Pallas kernels: 52.5 us -> 48 us
    pallas_call x1, Pallas kernels: 52.5 us -> 48 us  [fused(): pl.pallas_call(layer_kernel, out_shape=jax.ShapeDtypeStruct(queries.shape...]
where the time goes in v3:
time: 49.7 us; the launch traced here: 49.5 us
  Pallas kernels  48 us (97%)
  local copies, waits for them, and re-layouts  1.54 us (3%)
    pallas_call x1, Pallas kernels, fused(): pl.pallas_call(layer_kernel, out_shape=jax.ShapeDtypeStruct(queries.shape...  48 us
    unnamed x1, local copies, waits for them, and re-layouts  1.54 us

profile of v3, /device:TPU:0, one launch (start us, length us, event | category | flops | bytes accessed | tf_op | source)
XLA Modules:
  0.0 49.5 jit_solution(6934076360727469581)
XLA Ops:
  0.0 48.0 %shard_map.100 = bf16[8,6144]{1,0:T(8,128)(2,1)} custom-call(s32[8]{0:T(128)} %lengths.1, s32[1,2]{1,0:T(1,128)} %handoff.1, s32[8]{0:T(128)} %bitcast.3, bf16[8,6144]{1,0:T(8,128)(2,1)} %q_ref.1, bf16[6144]{0:T(1024)(128)(2,1)} %gain_ref.1, bf16[2,6144]{1,0:T(2,128)(2,1)} %bitcast.2, bf16[8,48,2048]{2,1,0:T(8,128)(2,1)} %kv_hbm.1, ...), custom_call_target="tpu_custom_call" | custom-call | flops 4831838208 | bytes 37748736 | tf_op jit(solution)/shard_map/pallas_call | solution.py:364
  48.0 1.5 %copy.12 = bf16[8,6144]{1,0:T(8,128)(2,1)} copy(bf16[8,6144]{1,0:T(8,128)(2,1)} %shard_map.100) | data formatting | bytes 196608

commit v4 on v3

--- a/solution.py
+++ b/solution.py
@@ -256,7 +256,7 @@
         )
 
     def first_copy(j):
-        if j % 3 != 2:
+        if j % 3 != 1:
             return remote(
                 sum_core.at[j, 1 - y], from_first.at[j], r_send.at[1, j], r_recv.at[1, j], across
             )
@@ -265,7 +265,7 @@
         )
 
     def second_copy(j):
-        if j % 3 != 2:
+        if j % 3 != 1:
             return remote(
                 sum_first.at[j, 1 - zp], from_second.at[j], r_send.at[2, j], r_recv.at[2, j], beside
             )
@@ -291,13 +291,13 @@
 
     def add_first(j):
         first_copy(j).wait_recv()
-        mine = sum_core[j, y] if j % 3 != 2 else sum_core[j, :, zp]
+        mine = sum_core[j, y] if j % 3 != 1 else sum_core[j, :, zp]
         sum_first[j] = (mine.astype(F32) + from_first[j].astype(F32)).astype(BF16)
         second_copy(j).start()
 
     def add_second(j):
         second_copy(j).wait_recv()
-        mine = sum_first[j, zp] if j % 3 != 2 else sum_first[j, y]
+        mine = sum_first[j, zp] if j % 3 != 1 else sum_first[j, y]
         total = mine.astype(F32) + from_second[j].astype(F32)
         upper = zh == 1
         own_sum[j] = jnp.where(upper, total[ROWS:], total[:ROWS])

time: 49.7 us -> 48.9 us (0.984)
  Pallas kernels: 48 us -> 47.2 us
    pallas_call x1, Pallas kernels: 48 us -> 47.2 us  [fused(): pl.pallas_call(layer_kernel, out_shape=jax.ShapeDtypeStruct(queries.shape...]
where the time goes in v4:
time: 48.9 us; the launch traced here: 48.8 us
  Pallas kernels  47.2 us (97%)
  local copies, waits for them, and re-layouts  1.54 us (3%)
    pallas_call x1, Pallas kernels, fused(): pl.pallas_call(layer_kernel, out_shape=jax.ShapeDtypeStruct(queries.shape...  47.2 us
    unnamed x1, local copies, waits for them, and re-layouts  1.54 us

profile of v4, /device:TPU:0, one launch (start us, length us, event | category | flops | bytes accessed | tf_op | source)
XLA Modules:
  0.0 48.8 jit_solution(8523077329894107067)
XLA Ops:
  0.0 47.2 %shard_map.100 = bf16[8,6144]{1,0:T(8,128)(2,1)} custom-call(s32[8]{0:T(128)} %lengths.1, s32[1,2]{1,0:T(1,128)} %handoff.1, s32[8]{0:T(128)} %bitcast.3, bf16[8,6144]{1,0:T(8,128)(2,1)} %q_ref.1, bf16[6144]{0:T(1024)(128)(2,1)} %gain_ref.1, bf16[2,6144]{1,0:T(2,128)(2,1)} %bitcast.2, bf16[8,48,2048]{2,1,0:T(8,128)(2,1)} %kv_hbm.1, ...), custom_call_target="tpu_custom_call" | custom-call | flops 4831838208 | bytes 37748736 | tf_op jit(solution)/shard_map/pallas_call | solution.py:364
  47.2 1.5 %copy.12 = bf16[8,6144]{1,0:T(8,128)(2,1)} copy(bf16[8,6144]{1,0:T(8,128)(2,1)} %shard_map.100) | data formatting | bytes 196608
